TPU v7x, 32 devices: a whole 2x2x4 slice. The times are simulated.
32 devices in a mesh: grp: 4 (over y, x), blk: 2 (over core), head: 4 (over z).
Axes of the slice: x: 2, y: 2, z: 4, core: 2. Of those that a mesh axis runs over, the one named last changes fastest.
Arguments:
- queries: bfloat16 [4096, 1024], P(('grp', 'blk', 'head')), may hold values from -6 to 6
- keys: bfloat16 [4096, 1024], P(('grp', 'blk', 'head')), may hold values from -6 to 6
- values: bfloat16 [4096, 1024], P(('grp', 'blk', 'head')), may hold values from -6 to 6
- out_grad: bfloat16 [4096, 1024], P(('grp', 'blk', 'head')), may hold values from -6 to 6
- segment: int32 [4096], P(('grp', 'blk', 'head')), may hold values from 0 to 3, never falling along the last dimension, each value on 1 to 2048 neighbouring positions
Outputs:
- attention_out: bfloat16 [4096, 1024], P(('grp', 'blk', 'head'))
- query_grad: bfloat16 [4096, 1024], P(('grp', 'blk', 'head'))
- key_grad: bfloat16 [4096, 1024], P(('grp', 'blk', 'head'))
- value_grad: bfloat16 [4096, 1024], P(('grp', 'blk', 'head'))
Inputs may be any that keep to these rules, and one draw needn't show every extreme that they name: `segment`: never falls along the pack; every stream covers 1 to 2048 consecutive positions and one covers exactly 2048.
All inputs are finite; a program needn't handle non-finite values.
Results may differ from a plain program's by a relative error of at most 0.0049.
Values may be sent and summed in bfloat16 or wider, within the bound.
No kernel may reach another device: no remote copies, remote signals or barrier semaphores. Data moves between devices by JAX's collectives and lax.ppermute only.
A program may use at most 64 MiB of HBM per device.

v0:
```python
import functools
import math

import jax
import jax.numpy as jnp
from jax import lax
from jax.experimental import pallas as pl
from jax.experimental.pallas import tpu as pltpu
from jax.sharding import Mesh, PartitionSpec as P

DH = 128
REACH = 4
PAIR = 2
CORE = 2
ROWS = 512
COLS = 512
STRIP = 32
PART = 128
MASKED = -1e6
CLEAR, MIXED = 0, 1
DEVICE_AXES = ("sup", "pair", "core", "head")
HEAD_AXES = ("head", "pair")
SEG_ROWS = 16
TAG_FLOPS = 40_000_000_000
ATTEND_VMEM = 24 * 1024 * 1024
MOVE_VMEM = 8 * 1024 * 1024
PACK_VMEM = 63 * 1024 * 1024


def run_copies(copies):
    for copy in copies:
        copy.start()
    for copy in copies:
        copy.wait()


def pack_kernel(queries, keys, values, out_grad, segment, packed, *scratch):
    held, numbers, places, sems = scratch[:4], *scratch[4:]
    heads = packed.shape[0]
    tokens = queries.shape[0]

    def copies_in(order):
        return [
            pltpu.make_async_copy(source, held[slot], sems.at[0, slot])
            for slot, source in enumerate(order)
        ]

    def start(order):
        for copy in copies_in(order):
            copy.start()

    first_keys = lax.axis_index("sup") % 2 == 0
    by_keys, by_queries = (keys, values, queries, out_grad), (queries, out_grad, keys, values)
    numbers_in = pltpu.make_async_copy(segment, numbers, sems.at[0, 4])
    numbers_in.start()

    @pl.when(first_keys)
    def _():
        start(by_keys)

    @pl.when(jnp.logical_not(first_keys))
    def _():
        start(by_queries)

    def copy_out(part, at, rows):
        rows = pl.ds(at, rows)
        return pltpu.make_async_copy(places.at[:, rows], packed.at[:, rows], sems.at[1, part])

    numbers_in.wait()
    places[:, pl.ds(2 * tokens, SEG_ROWS)] = jnp.broadcast_to(
        (numbers[...] + 1).astype(jnp.float32).astype(places.dtype)[None], (heads, SEG_ROWS, tokens)
    )
    outs = []
    for slot, copy_in in enumerate(copies_in(by_keys)):
        copy_in.wait()
        at = slot * tokens + (SEG_ROWS if slot > 1 else 0)
        for head in range(heads):
            places[head, pl.ds(at, tokens)] = held[slot][:, pl.ds(head * DH, DH)]
        outs.append(copy_out(slot, at, tokens + (SEG_ROWS if slot == 1 else 0)))
        outs[-1].start()
    for copy in outs:
        copy.wait()


def pack(queries, keys, values, out_grad, segment):
    tokens, features = queries.shape
    shape = (features // DH, 4 * tokens + SEG_ROWS, DH)
    anywhere = pl.BlockSpec(memory_space=pl.ANY)
    return pl.pallas_call(
        pack_kernel,
        out_shape=jax.ShapeDtypeStruct(shape, queries.dtype),
        in_specs=[anywhere] * 5,
        out_specs=anywhere,
        scratch_shapes=[pltpu.VMEM(queries.shape, queries.dtype)] * 4
        + [
            pltpu.VMEM(segment.shape, segment.dtype),
            pltpu.VMEM(shape, queries.dtype),
            pltpu.SemaphoreType.DMA((2, 5)),
        ],
        compiler_params=pltpu.CompilerParams(vmem_limit_bytes=PACK_VMEM),
    )(queries, keys, values, out_grad, segment)


def unpack_kernel(queries_on, back, *refs):
    outs, rows_out, sems = refs[-6:-2], refs[-2], refs[-1]
    heads = back.shape[0]
    tokens = rows_out.shape[1]
    of_queries = lax.axis_index("sup") % 2 == queries_on

    def copy_out(slot, target):
        return pltpu.make_async_copy(rows_out.at[slot], target, sems.at[slot])

    for slot, (by_query, by_key) in enumerate(((outs[0], outs[3]), (outs[1], outs[2]))):
        for head in range(heads):
            rows_out[slot, :, pl.ds(head * DH, DH)] = back[head, pl.ds(slot * tokens, tokens)]
        pl.when(of_queries)(lambda: copy_out(slot, by_query).start())
        pl.when(jnp.logical_not(of_queries))(lambda: copy_out(slot, by_key).start())
    for slot in range(2):
        copy_out(slot, outs[slot]).wait()


def unpack(queries_on, back, outs=()):
    heads, rows, _ = back.shape
    tokens = rows // 2
    anywhere = pl.BlockSpec(memory_space=pl.ANY)
    return pl.pallas_call(
        functools.partial(unpack_kernel, queries_on),
        out_shape=[jax.ShapeDtypeStruct((tokens, heads * DH), back.dtype)] * 4,
        in_specs=[pl.BlockSpec(memory_space=pltpu.VMEM)] + [anywhere] * len(outs),
        out_specs=[anywhere] * 4,
        scratch_shapes=[
            pltpu.VMEM((2, tokens, heads * DH), back.dtype),
            pltpu.SemaphoreType.DMA((2,)),
        ],
        input_output_aliases={1 + i: i for i in range(len(outs))},
        compiler_params=pltpu.CompilerParams(vmem_limit_bytes=MOVE_VMEM),
    )(back, *outs)


def tag_kernel(given, other, tag):
    tag[...] = given[...]


def later_tag(tag, other):
    vmem = pl.BlockSpec(memory_space=pltpu.VMEM)
    return pl.pallas_call(
        tag_kernel,
        out_shape=jax.ShapeDtypeStruct(tag.shape, tag.dtype),
        in_specs=[vmem, pl.BlockSpec(memory_space=pl.ANY)],
        out_specs=vmem,
        compiler_params=pltpu.CompilerParams(vmem_limit_bytes=MOVE_VMEM),
        cost_estimate=pl.CostEstimate(
            flops=TAG_FLOPS, bytes_accessed=2 * tag.size, transcendentals=0
        ),
    )(tag, other)


def attend_kernel(factors, slabs, forward, own_seg, other_seg, rows_slab, *refs):
    score_scale, norm = factors
    col_slabs = refs[: 2 * slabs]
    packed, *tag = refs[2 * slabs : -11]
    seg, seg_rows, seg_cols, row_one, row_two, col_one, col_two = refs[-11:-4]
    sum_one, sum_two, work, sem = refs[-4:]
    parity, core = lax.axis_index("sup") % 2, lax.axis_index("core")
    sign = (1 - 2 * parity) * (1 if forward else -1)
    chunks = rows_slab.shape[0]
    tokens = packed.shape[1] // 2
    half_rows = chunks // PAIR * tokens
    half_blocks = half_rows // COLS
    local_blocks = REACH * half_blocks
    row_blocks = chunks * tokens // ROWS
    col_chunks = COLS // tokens
    if tag:
        tag[0][...] = jnp.zeros_like(tag[0])

    def place_of(index, chunk):
        slab, owner = index // 2, (core if index % 2 == 0 else 1 - core)
        inner, pair = chunk // PAIR, chunk % PAIR
        return (slab * REACH + pair * CORE + owner) * (chunks // PAIR) + inner

    def row_of(chunk):
        return (chunk % PAIR * (chunks // PAIR) + chunk // PAIR) * tokens

    for index, source in enumerate(col_slabs):
        source, at = (source, 2 * tokens) if index > 1 else ((own_seg, other_seg)[index], 0)
        for chunk in range(chunks):
            numbers = source[chunk, pl.ds(at, SEG_ROWS)].astype(jnp.float32)[:1]
            place = place_of(index, chunk)
            lanes = pl.ds(chunk // PAIR % col_chunks * tokens, tokens)
            seg_cols[place // col_chunks, :, lanes] = numbers.astype(jnp.int32)
    to_scalars = pltpu.make_async_copy(seg_cols, seg, sem)
    to_scalars.start()
    for index, source in enumerate(col_slabs):
        for chunk in range(chunks):
            place = place_of(index, chunk)
            rows = pl.ds(chunk // PAIR % col_chunks * tokens, tokens)
            for slot, ref in enumerate((col_one, col_two)):
                ref[place // col_chunks, rows] = source[chunk, pl.ds(slot * tokens, tokens)]
    for chunk in range(chunks):
        for slot, ref in enumerate((row_one, row_two)):
            ref[pl.ds(row_of(chunk), tokens)] = rows_slab[chunk, pl.ds(slot * tokens, tokens)]

    def row_token_of(row_block):
        row_start = row_block * ROWS
        return (row_start // half_rows * CORE + core) * half_rows + row_start % half_rows

    def col_token_of(block):
        beyond = jnp.where(block >= local_blocks, 1, 0)
        return block * COLS - beyond * (sign + 1) * local_blocks * COLS

    def seg_at(token):
        return seg[token // COLS, 0, token % COLS]

    sum_one[...] = jnp.zeros_like(sum_one)
    sum_two[...] = jnp.zeros_like(sum_two)
    to_scalars.wait()
    total = 0
    for row_block in range(row_blocks):
        row_token = row_token_of(row_block)
        row_first, row_last = seg_at(row_token), seg_at(row_token + ROWS - 1)
        at_rows = row_block * ROWS

        @pl.when(row_first == row_last)
        def _():
            seg_rows[pl.ds(at_rows, ROWS)] = jnp.full((ROWS, DH), row_first, jnp.int32)

        @pl.when(row_first != row_last)
        def _():
            for chunk in range(chunks):
                if row_of(chunk) // ROWS != row_block:
                    continue
                numbers = own_seg[chunk].astype(jnp.float32)[:1]
                seg_rows[pl.ds(row_of(chunk), tokens)] = jnp.transpose(
                    jnp.broadcast_to(numbers, (DH, tokens))
                ).astype(jnp.int32)

        for block in range(slabs * local_blocks):
            col_token = col_token_of(block)
            col_first, col_last = seg[block, 0, 0], seg[block, 0, COLS - 1]
            touching = (col_last >= row_first) & (col_first <= row_last)
            ahead, behind = col_token - row_token, row_token + ROWS - col_token
            reached = jnp.where(sign > 0, behind > 0, ahead + COLS > 0)
            inside = jnp.where(sign > 0, ahead + COLS <= 1, behind <= 1)
            same = (row_first == row_last) & (col_first == row_first) & (col_last == row_first)
            work[0, total] = row_block
            work[1, total] = block
            work[2, total] = jnp.where(same & inside, CLEAR, MIXED)
            total = total + jnp.where(touching & reached, 1, 0)
    dims = (((1,), (1,)), ((), ()))

    def weigh(raw, dprob):
        logistic = pltpu.reciprocal(
            1.0 + jnp.exp2(raw * (-score_scale * math.log2(math.e))), approx=True
        )
        active = raw * logistic
        slope = logistic + active * score_scale * (1.0 - logistic)
        return (active * (score_scale * norm)).astype(jnp.bfloat16), (dprob * slope).astype(
            jnp.bfloat16
        )

    def tile(item, masked):
        row_block, block = work[0, item], work[1, item]
        if masked:
            offset = (col_token_of(block) - row_token_of(row_block)) * sign
            distance = (
                lax.broadcasted_iota(jnp.int32, (STRIP, DH), 0)
                - lax.broadcasted_iota(jnp.int32, (STRIP, DH), 1)
            ) * sign

        def products(part):
            at = pl.ds(pl.multiple_of(row_block * ROWS + part, PART), PART)
            return [
                lax.dot_general(rows[at], cols[block], dims, preferred_element_type=jnp.float32)
                for rows, cols in ((row_one, col_one), (row_two, col_two))
            ]

        ahead = products(0)
        for part in range(0, ROWS, PART):
            scores, dprobs = ahead
            if part + PART < ROWS:
                ahead = products(part + PART)
            weights, dscores = [], []
            for row in range(0, PART, STRIP):
                pieces = []
                if masked:
                    row_seg = seg_rows[pl.ds(row_block * ROWS + part + row, STRIP)]
                for col in range(0, COLS, DH):
                    raw = scores[row : row + STRIP, col : col + DH]
                    if masked:
                        col_seg = jnp.broadcast_to(seg_cols[block, :, pl.ds(col, DH)], (STRIP, DH))
                        allowed = (row_seg == col_seg) & (
                            distance >= offset - (part + row - col) * sign
                        )
                        raw = jnp.where(allowed, raw, MASKED)
                    pieces.append(weigh(raw, dprobs[row : row + STRIP, col : col + DH]))
                weights.append(jnp.concatenate([piece[0] for piece in pieces], axis=1))
                dscores.append(jnp.concatenate([piece[1] for piece in pieces], axis=1))
            for target, left, cols in ((sum_one, weights, col_two), (sum_two, dscores, col_one)):
                target[row_block, pl.ds(part, PART)] += jnp.dot(
                    jnp.concatenate(left, axis=0), cols[block], preferred_element_type=jnp.float32
                )

    def step(item, carry):
        clear = work[2, item] == CLEAR
        pl.when(clear)(functools.partial(tile, item, False))
        pl.when(jnp.logical_not(clear))(functools.partial(tile, item, True))
        return carry

    lax.fori_loop(0, total, step, 0)
    for chunk in range(chunks):
        row_block, inner = row_of(chunk) // ROWS, row_of(chunk) % ROWS
        at = pl.ds(inner, tokens)
        packed[chunk, pl.ds(0, tokens)] = sum_one[row_block, at].astype(packed.dtype)
        packed[chunk, pl.ds(tokens, tokens)] = (
            sum_two[row_block, at] * (norm * score_scale)
        ).astype(packed.dtype)


def attend(forward, rows_slab, col_slabs, local_segs):
    chunks = rows_slab.shape[0]
    rows = chunks * DH
    slabs = len(col_slabs) // 2
    reach = CORE * rows
    factors = (1.0 / math.sqrt(DH), 1.0 / math.sqrt(reach))
    vmem = pl.BlockSpec(memory_space=pltpu.VMEM)
    dtype = rows_slab.dtype
    blocks = slabs * reach // COLS
    row_blocks = rows // ROWS
    sums = jax.ShapeDtypeStruct((chunks, 2 * rows // chunks, DH), dtype)
    tag = [jax.ShapeDtypeStruct((1, 1, DH), jnp.float32)] if forward else []
    return pl.pallas_call(
        functools.partial(attend_kernel, factors, slabs, forward),
        out_shape=[sums] + tag,
        in_specs=[vmem] * (3 + 2 * slabs),
        out_specs=[vmem] * (1 + len(tag)),
        scratch_shapes=[
            pltpu.SMEM((blocks, 1, COLS), jnp.int32),
            pltpu.VMEM((rows, DH), jnp.int32),
            pltpu.VMEM((blocks, 1, COLS), jnp.int32),
            pltpu.VMEM((rows, DH), dtype),
            pltpu.VMEM((rows, DH), dtype),
            pltpu.VMEM((blocks, COLS, DH), dtype),
            pltpu.VMEM((blocks, COLS, DH), dtype),
        ]
        + [
            pltpu.VMEM((row_blocks, ROWS, DH), jnp.float32),
            pltpu.VMEM((row_blocks, ROWS, DH), jnp.float32),
            pltpu.SMEM((3, row_blocks * blocks + 1), jnp.int32),
            pltpu.SemaphoreType.DMA(()),
        ],
        compiler_params=pltpu.CompilerParams(vmem_limit_bytes=ATTEND_VMEM),
        cost_estimate=pl.CostEstimate(
            flops=8 * DH * rows * reach * slabs if forward else 0,
            bytes_accessed=8 * rows_slab.size if forward else 0,
            transcendentals=rows * reach * slabs if forward else 0,
        ),
    )(*local_segs, rows_slab, *col_slabs)


def shards(queries, keys, values, out_grad, segment):
    sups = lax.axis_size("sup")
    tokens = queries.shape[0]

    def over_heads(packed):
        return lax.all_to_all(packed, HEAD_AXES, split_axis=0, concat_axis=0, tiled=True)

    def with_other_core(slab):
        return [slab, lax.ppermute(slab, "core", [(0, 1), (1, 0)])]

    def over_sups(slab, start):
        pairs = [(i, i + 1) for i in range(start, sups - 1, 2)]
        return lax.ppermute(slab, "sup", pairs + [(b, a) for a, b in pairs])

    slab = over_heads(pack(queries, keys, values, out_grad, segment[None]))
    first_own, second_own = slab[:, : 2 * tokens + SEG_ROWS], slab[:, 2 * tokens + SEG_ROWS :]
    first_cols = with_other_core(first_own)
    beyond = over_sups(first_own, 0)
    second_cols = with_other_core(second_own)
    local_segs = [slab[:, 2 * tokens :] for slab in first_cols]
    first_all = first_cols
    if sups > 2:
        later = over_sups(jnp.concatenate([second_own, local_segs[0]], axis=1), 1)
        first_all = first_cols + with_other_core(later)
    first_sums, tag = attend(True, second_own, first_all, local_segs)
    first_back = over_heads(first_sums)
    beyond_cols = with_other_core(beyond + later_tag(tag, second_cols[1]).astype(beyond.dtype))
    (second_sums,) = attend(False, first_own, second_cols + beyond_cols, local_segs)
    second_back = over_heads(second_sums)
    return tuple(unpack(1, second_back, unpack(0, first_back)))


def solution(mesh):
    blocks = mesh.shape["grp"] * mesh.shape["blk"]
    grid = Mesh(
        mesh.devices.reshape(blocks // REACH, PAIR, CORE, mesh.shape["head"]), DEVICE_AXES
    )
    rows = P(DEVICE_AXES, None)
    return jax.shard_map(
        shards,
        mesh=grid,
        in_specs=(rows, rows, rows, rows, P(DEVICE_AXES)),
        out_specs=(rows, rows, rows, rows),
        check_vma=False,
    )
```

profile of v0, /device:TPU:0, one launch (start us, length us, event | category | flops | bytes accessed | tf_op | source)
XLA Modules:
  0.0 84.2 jit_solution(4682280775063638737)
XLA Ops:
  0.6 2.1 %shard_map.84 = bf16[8,528,128]{2,1,0:T(8,128)(2,1)} custom-call(bf16[128,1024]{1,0:T(8,128)(2,1)} %queries.1, bf16[128,1024]{1,0:T(8,128)(2,1)} %keys.1, bf16[128,1024]{1,0:T(8,128)(2,1)} %values.1, bf16[128,1024]{1,0:T(8,128)(2,1)} %out_grad.1, s32[1,128]{1,0:T(1,128)} %bitcast.3), custom_call_target="tpu_custom_call" | custom-call | tf_op jit(solution)/shard_map/pallas_call | solution.py:89
  2.7 34.5 %all_to_all.15 = bf16[8,528,128]{2,1,0:T(8,128)(2,1)S(1)} all-to-all(bf16[8,528,128]{2,1,0:T(8,128)(2,1)} %shard_map.84), channel_id=1, replica_groups=mesh['sup'=2,'pair'=2,'core'=2,'head'=4] {'head','pair'}, dimensions={0} | all-to-all | bytes 2162688 | tf_op jit(solution)/shard_map/all_to_all | solution.py:365
  37.3 0.1 collective-permute-start
  37.4 0.6 collective-permute-start.1
  38.0 1.5 %collective-permute-start.2 = (bf16[8,272,128]{2,1,0:T(8,128)(2,1)S(1)}, bf16[8,272,128]{2,1,0:T(8,128)(2,1)S(1)}, u32[]{:S(2)}, u32[]{:S(2)}) collective-permute-start(bf16[8,272,128]{2,1,0:T(8,128)(2,1)S(1)} %slice.18.refs_0_.rows_slab), channel_id=1, source_target_pairs={{0,16},{16,0},{1,17},{17,1},{2,18},{18,2},{3,19},{19,3},{4,20},{20... | collective-permute-start | bytes 1671176 | tf_op jit(solution)/shard_map/ppermute | solution.py:372
  39.5 0.0 collective-permute-done.refs_1_
  39.5 5.2 %shard_map.85 = (bf16[8,256,128]{2,1,0:T(8,128)(2,1)}, f32[1,1,128]{2,1,0:T(1,128)S(1)}) custom-call(bf16[8,16,128]{2,1,0:T(8,128)(2,1)S(1)} %slice.17.own_seg, bf16[8,16,128]{2,1,0:T(8,128)(2,1)S(1)} %slice.19.other_seg, bf16[8,256,128]{2,1,0:T(8,128)(2,1)S(1)} %slice.20.rows_slab.refs_0_, bf16[8,272,128]{2,1,0:T(8,128)(2,1)S(1)} %slice.18.refs_0_.rows_slab, ...), custom_call_target="tpu_custom_call" | custom-call | flops 2147483648 | bytes 2097152 | tf_op jit(solution)/shard_map/pallas_call | solution.py:331
  44.7 3.5 %all-to-all-start.2 = ((bf16[8,256,128]{2,1,0:T(8,128)(2,1)}), bf16[8,256,128]{2,1,0:T(8,128)(2,1)S(1)}, u32[]{:S(2)}, u32[]{:S(2)}) async-start(bf16[8,256,128]{2,1,0:T(8,128)(2,1)} %get-tuple-element.11), calls=%async_computation.2 | async-start | bytes 1048576 | tf_op jit(solution)/shard_map/all_to_all | solution.py:365
  48.3 0.0 collective-permute-done.1.other.refs_1_
  48.3 4.3 %collective-permute-done.2 = bf16[8,272,128]{2,1,0:T(8,128)(2,1)S(1)} collective-permute-done((bf16[8,272,128]{2,1,0:T(8,128)(2,1)S(1)}, bf16[8,272,128]{2,1,0:T(8,128)(2,1)S(1)}, u32[]{:S(2)}, u32[]{:S(2)}) %collective-permute-start.2) | collective-permute-done | bytes 557088 | tf_op jit(solution)/shard_map/ppermute | solution.py:372
  52.6 0.1 collective-permute-start.3
  52.7 1.9 %collective-permute-done.3.refs_3_ = bf16[8,272,128]{2,1,0:T(8,128)(2,1)S(1)} collective-permute-done((bf16[8,272,128]{2,1,0:T(8,128)(2,1)S(1)}, bf16[8,272,128]{2,1,0:T(8,128)(2,1)S(1)}, u32[]{:S(2)}, u32[]{:S(2)}) %collective-permute-start.3) | collective-permute-done | bytes 557088 | tf_op jit(solution)/shard_map/ppermute | solution.py:368
  54.6 8.5 %shard_map.87 = bf16[8,256,128]{2,1,0:T(8,128)(2,1)} custom-call(bf16[8,16,128]{2,1,0:T(8,128)(2,1)S(1)} %slice.17.own_seg, bf16[8,16,128]{2,1,0:T(8,128)(2,1)S(1)} %slice.19.other_seg, bf16[8,272,128]{2,1,0:T(8,128)(2,1)S(1)} %slice.18.refs_0_.rows_slab, bf16[8,256,128]{2,1,0:T(8,128)(2,1)S(1)} %slice.20.rows_slab.refs_0_, ...), custom_call_target="tpu_custom_call" | custom-call | tf_op jit(solution)/shard_map/pallas_call | solution.py:331
  63.1 0.0 all-to-all-done.2.back
  63.1 4.5 %all-to-all-start.1 = ((bf16[8,256,128]{2,1,0:T(8,128)(2,1)}), bf16[8,256,128]{2,1,0:T(8,128)(2,1)S(1)}, u32[]{:S(2)}, u32[]{:S(2)}) async-start(bf16[8,256,128]{2,1,0:T(8,128)(2,1)} %shard_map.87), calls=%async_computation.1 | async-start | bytes 1048576 | tf_op jit(solution)/shard_map/all_to_all | solution.py:365
  67.6 0.9 %shard_map.88 = (bf16[128,1024]{1,0:T(8,128)(2,1)}, bf16[128,1024]{1,0:T(8,128)(2,1)}, bf16[128,1024]{1,0:T(8,128)(2,1)}, bf16[128,1024]{1,0:T(8,128)(2,1)}) custom-call(bf16[8,256,128]{2,1,0:T(8,128)(2,1)S(1)} %all-to-all-done.2.back), custom_call_target="tpu_custom_call" | custom-call | tf_op jit(solution)/shard_map/pallas_call | solution.py:126
  68.5 14.8 %all-to-all-done.1.back = bf16[8,256,128]{2,1,0:T(8,128)(2,1)S(1)} async-done(((bf16[8,256,128]{2,1,0:T(8,128)(2,1)}), bf16[8,256,128]{2,1,0:T(8,128)(2,1)S(1)}, u32[]{:S(2)}, u32[]{:S(2)}) %all-to-all-start.1) | async-done | bytes 524320 | tf_op jit(solution)/shard_map/all_to_all | solution.py:365
  83.3 0.9 %shard_map.89 = (bf16[128,1024]{1,0:T(8,128)(2,1)}, bf16[128,1024]{1,0:T(8,128)(2,1)}, bf16[128,1024]{1,0:T(8,128)(2,1)}, bf16[128,1024]{1,0:T(8,128)(2,1)}) custom-call(bf16[8,256,128]{2,1,0:T(8,128)(2,1)S(1)} %all-to-all-done.1.back, ...), custom_call_target="tpu_custom_call", output_to_operand_aliasing={{0}: (1, {}), {1}: (2, {}), {2}: (3, {}), {3}: (4, {})} | custom-call | tf_op jit(solution)/shard_map/pallas_call | solution.py:126
  (7 shorter events, 0.1 us)
Async XLA Ops:
  37.3 2.2 %collective-permute-start = (bf16[8,272,128]{2,1,0:T(8,128)(2,1)S(1)}, bf16[8,272,128]{2,1,0:T(8,128)(2,1)S(1)}, u32[]{:S(2)}, u32[]{:S(2)}) collective-permute-start(bf16[8,272,128]{2,1,0:T(8,128)(2,1)S(1)} %slice.18.refs_0_.rows_slab), channel_id=1, source_target_pairs={{0,4},{4,0},{1,5},{5,1},{2,6},{6,2},{3,7},{7,3},{8,12},{12,8},{9,1... | collective-permute-start | bytes 1671176 | tf_op jit(solution)/shard_map/ppermute | solution.py:368
  37.4 10.9 %collective-permute-start.1 = (bf16[8,256,128]{2,1,0:T(8,128)(2,1)S(1)}, bf16[8,256,128]{2,1,0:T(8,128)(2,1)S(1)}, u32[]{:S(2)}, u32[]{:S(2)}) collective-permute-start(bf16[8,256,128]{2,1,0:T(8,128)(2,1)S(1)} %slice.20.rows_slab.refs_0_), channel_id=1, source_target_pairs={{0,4},{4,0},{1,5},{5,1},{2,6},{6,2},{3,7},{7,3},{8,12},{12,8},{9,1... | collective-permute-start | bytes 1572872 | tf_op jit(solution)/shard_map/ppermute | solution.py:368
  38.0 14.6 %collective-permute-start.2 = (bf16[8,272,128]{2,1,0:T(8,128)(2,1)S(1)}, bf16[8,272,128]{2,1,0:T(8,128)(2,1)S(1)}, u32[]{:S(2)}, u32[]{:S(2)}) collective-permute-start(bf16[8,272,128]{2,1,0:T(8,128)(2,1)S(1)} %slice.18.refs_0_.rows_slab), channel_id=1, source_target_pairs={{0,16},{16,0},{1,17},{17,1},{2,18},{18,2},{3,19},{19,3},{4,20},{20... | collective-permute-start | bytes 1671176 | tf_op jit(solution)/shard_map/ppermute | solution.py:372
  44.7 18.4 %all-to-all-start.2 = ((bf16[8,256,128]{2,1,0:T(8,128)(2,1)}), bf16[8,256,128]{2,1,0:T(8,128)(2,1)S(1)}, u32[]{:S(2)}, u32[]{:S(2)}) async-start(bf16[8,256,128]{2,1,0:T(8,128)(2,1)} %get-tuple-element.11), calls=%async_computation.2 | async-start | bytes 1048576 | tf_op jit(solution)/shard_map/all_to_all | solution.py:365
  52.6 2.0 %collective-permute-start.3 = (bf16[8,272,128]{2,1,0:T(8,128)(2,1)S(1)}, bf16[8,272,128]{2,1,0:T(8,128)(2,1)S(1)}, u32[]{:S(2)}, u32[]{:S(2)}) collective-permute-start(bf16[8,272,128]{2,1,0:T(8,128)(2,1)S(1)} %broadcast_add_fusion.refs_2_), channel_id=1, source_target_pairs={{0,4},{4,0},{1,5},{5,1},{2,6},{6,2},{3,7},{7,3},{8,12},{12,8},{9,1... | collective-permute-start | bytes 1671176 | tf_op jit(solution)/shard_map/ppermute | solution.py:368
  63.1 20.1 %all-to-all-start.1 = ((bf16[8,256,128]{2,1,0:T(8,128)(2,1)}), bf16[8,256,128]{2,1,0:T(8,128)(2,1)S(1)}, u32[]{:S(2)}, u32[]{:S(2)}) async-start(bf16[8,256,128]{2,1,0:T(8,128)(2,1)} %shard_map.87), calls=%async_computation.1 | async-start | bytes 1048576 | tf_op jit(solution)/shard_map/all_to_all | solution.py:365
where the time goes:
time: 84.6 us; the launch traced here: 84.2 us
  blocking collectives  34.5 us (41%)
  waiting for transfers between devices  21 us (25%)
  Pallas kernels  17.6 us (21%)
  starting transfers between devices  10.2 us (12%)
    all_to_all x1, blocking collectives, over_heads(): lax.all_to_all(packed, HEAD_AXES, split_axis=0, concat_axis=0, tiled=True)  34.5 us
    all_to_all x2, waiting for transfers between devices, over_heads(): lax.all_to_all(packed, HEAD_AXES, split_axis=0, concat_axis=0, tiled=True)  14.8 us
    pallas_call x2, Pallas kernels, attend(): pl.pallas_call(functools.partial(attend_kernel, factors, slabs, forward),...  13.7 us
    all_to_all x2, starting transfers between devices, over_heads(): lax.all_to_all(packed, HEAD_AXES, split_axis=0, concat_axis=0, tiled=True)  7.97 us
    ppermute x1, waiting for transfers between devices, over_sups(): return lax.ppermute(slab, 'sup', pairs + [(b, a) for a, b in pairs])  4.28 us
    pallas_call x1, Pallas kernels, pack(): pl.pallas_call(pack_kernel, out_shape=jax.ShapeDtypeStruct(shape, queries...  2.11 us
    ppermute x3, waiting for transfers between devices, with_other_core(): return [slab, lax.ppermute(slab, 'core', [(0, 1), (1, 0)])]  1.95 us
    pallas_call x2, Pallas kernels, unpack(): pl.pallas_call(functools.partial(unpack_kernel, queries_on), out_shape=[j...  1.77 us
  transfers between devices with their start and end apart: 6, of which 3 were waited for; matrix products, arithmetic and copies ran while one was open for 0% of the time, Pallas kernels for 17%

commit v1 on v0

--- a/solution.py
+++ b/solution.py
@@ -15,7 +15,7 @@
 ROWS = 512
 COLS = 512
 STRIP = 32
-PART = 128
+PART = 256
 MASKED = -1e6
 CLEAR, MIXED = 0, 1
 DEVICE_AXES = ("sup", "pair", "core", "head")
@@ -175,25 +175,26 @@
 
     def place_of(index, chunk):
         slab, owner = index // 2, (core if index % 2 == 0 else 1 - core)
-        inner, pair = chunk // PAIR, chunk % PAIR
+        inner, pair = divmod(chunks - 1 - chunk, PAIR)
         return (slab * REACH + pair * CORE + owner) * (chunks // PAIR) + inner
 
     def row_of(chunk):
-        return (chunk % PAIR * (chunks // PAIR) + chunk // PAIR) * tokens
+        inner, pair = divmod(chunks - 1 - chunk, PAIR)
+        return (pair * (chunks // PAIR) + inner) * tokens
 
     for index, source in enumerate(col_slabs):
         source, at = (source, 2 * tokens) if index > 1 else ((own_seg, other_seg)[index], 0)
         for chunk in range(chunks):
             numbers = source[chunk, pl.ds(at, SEG_ROWS)].astype(jnp.float32)[:1]
             place = place_of(index, chunk)
-            lanes = pl.ds(chunk // PAIR % col_chunks * tokens, tokens)
+            lanes = pl.ds(row_of(chunk) % COLS, tokens)
             seg_cols[place // col_chunks, :, lanes] = numbers.astype(jnp.int32)
     to_scalars = pltpu.make_async_copy(seg_cols, seg, sem)
     to_scalars.start()
     for index, source in enumerate(col_slabs):
         for chunk in range(chunks):
             place = place_of(index, chunk)
-            rows = pl.ds(chunk // PAIR % col_chunks * tokens, tokens)
+            rows = pl.ds(row_of(chunk) % COLS, tokens)
             for slot, ref in enumerate((col_one, col_two)):
                 ref[place // col_chunks, rows] = source[chunk, pl.ds(slot * tokens, tokens)]
     for chunk in range(chunks):
@@ -266,19 +267,12 @@
                 lax.broadcasted_iota(jnp.int32, (STRIP, DH), 0)
                 - lax.broadcasted_iota(jnp.int32, (STRIP, DH), 1)
             ) * sign
-
-        def products(part):
+        for part in range(0, ROWS, PART):
             at = pl.ds(pl.multiple_of(row_block * ROWS + part, PART), PART)
-            return [
+            scores, dprobs = [
                 lax.dot_general(rows[at], cols[block], dims, preferred_element_type=jnp.float32)
                 for rows, cols in ((row_one, col_one), (row_two, col_two))
             ]
-
-        ahead = products(0)
-        for part in range(0, ROWS, PART):
-            scores, dprobs = ahead
-            if part + PART < ROWS:
-                ahead = products(part + PART)
             weights, dscores = [], []
             for row in range(0, PART, STRIP):
                 pieces = []
@@ -362,7 +356,14 @@
     tokens = queries.shape[0]
 
     def over_heads(packed):
-        return lax.all_to_all(packed, HEAD_AXES, split_axis=0, concat_axis=0, tiled=True)
+        return lax.all_to_all(
+            packed,
+            HEAD_AXES,
+            split_axis=0,
+            concat_axis=0,
+            axis_index_groups=[list(range(packed.shape[0]))[::-1]],
+            tiled=True,
+        )
 
     def with_other_core(slab):
         return [slab, lax.ppermute(slab, "core", [(0, 1), (1, 0)])]

time: 84.6 us -> 84.6 us (level)
  starting transfers between devices: 10.2 us -> 16 us
  waiting for transfers between devices: 21 us -> 15.4 us
    all_to_all x2, starting transfers between devices: 7.97 us -> 12.6 us  [over_heads(): lax.all_to_all(packed, HEAD_AXES, split_axis=0, concat_axis=0, axis_index...]
    ppermute x1, waiting for transfers between devices: 4.28 us -> 0.49 us  [over_sups(): return lax.ppermute(slab, 'sup', pairs + [(b, a) for a, b in pairs])]
    all_to_all x2, waiting for transfers between devices: 14.8 us -> 13.4 us  [over_heads(): lax.all_to_all(packed, HEAD_AXES, split_axis=0, concat_axis=0, axis_index...]
    ppermute x3, starting transfers between devices: 0.7 us -> 1.86 us  [with_other_core(): return [slab, lax.ppermute(slab, 'core', [(0, 1), (1, 0)])]]
  transfers between devices with their start and end apart: 6 -> 6, of which waited for: 3 -> 4; matrix products, arithmetic and copies ran while one was open for 0% -> 0% of each run, Pallas kernels for 17% -> 18%
where the time goes in v1:
time: 84.6 us; the launch traced here: 84.1 us
  blocking collectives  33.8 us (40%)
  Pallas kernels  18 us (21%)
  starting transfers between devices  16 us (19%)
  waiting for transfers between devices  15.4 us (18%)
    all_to_all x1, blocking collectives, over_heads(): lax.all_to_all(packed, HEAD_AXES, split_axis=0, concat_axis=0, axis_index...  33.8 us
    pallas_call x2, Pallas kernels, attend(): pl.pallas_call(functools.partial(attend_kernel, factors, slabs, forward),...  14.1 us
    all_to_all x2, waiting for transfers between devices, over_heads(): lax.all_to_all(packed, HEAD_AXES, split_axis=0, concat_axis=0, axis_index...  13.4 us
    all_to_all x2, starting transfers between devices, over_heads(): lax.all_to_all(packed, HEAD_AXES, split_axis=0, concat_axis=0, axis_index...  12.6 us
    pallas_call x1, Pallas kernels, pack(): pl.pallas_call(pack_kernel, out_shape=jax.ShapeDtypeStruct(shape, queries...  2.11 us
    ppermute x3, starting transfers between devices, with_other_core(): return [slab, lax.ppermute(slab, 'core', [(0, 1), (1, 0)])]  1.86 us
    pallas_call x2, Pallas kernels, unpack(): pl.pallas_call(functools.partial(unpack_kernel, queries_on), out_shape=[j...  1.77 us
  transfers between devices with their start and end apart: 6, of which 4 were waited for; matrix products, arithmetic and copies ran while one was open for 0% of the time, Pallas kernels for 18%

profile of v1, /device:TPU:0, one launch (start us, length us, event | category | flops | bytes accessed | tf_op | source)
XLA Modules:
  0.0 84.1 jit_solution(10634245663001272178)
XLA Ops:
  0.6 2.1 %shard_map.84 = bf16[8,528,128]{2,1,0:T(8,128)(2,1)} custom-call(bf16[128,1024]{1,0:T(8,128)(2,1)} %queries.1, bf16[128,1024]{1,0:T(8,128)(2,1)} %keys.1, bf16[128,1024]{1,0:T(8,128)(2,1)} %values.1, bf16[128,1024]{1,0:T(8,128)(2,1)} %out_grad.1, s32[1,128]{1,0:T(1,128)} %bitcast.3), custom_call_target="tpu_custom_call" | custom-call | tf_op jit(solution)/shard_map/pallas_call | solution.py:89
  2.7 33.8 %all_to_all.15 = bf16[8,528,128]{2,1,0:T(8,128)(2,1)S(1)} all-to-all(bf16[8,528,128]{2,1,0:T(8,128)(2,1)} %shard_map.84), channel_id=1, replica_groups={{11,3,10,2,9,1,8,0},{15,7,14,6,13,5,12,4},{27,19,26,18,25,17,24,16},{31..., dimensions={0} | all-to-all | bytes 2162688 | tf_op jit(solution)/shard_map/all_to_all | solution.py:359
  36.6 0.1 collective-permute-start
  36.7 0.6 collective-permute-start.1
  37.2 1.5 %collective-permute-start.2 = (bf16[8,272,128]{2,1,0:T(8,128)(2,1)S(1)}, bf16[8,272,128]{2,1,0:T(8,128)(2,1)S(1)}, u32[]{:S(2)}, u32[]{:S(2)}) collective-permute-start(bf16[8,272,128]{2,1,0:T(8,128)(2,1)S(1)} %slice.18.refs_0_.rows_slab), channel_id=1, source_target_pairs={{0,16},{16,0},{1,17},{17,1},{2,18},{18,2},{3,19},{19,3},{4,20},{20... | collective-permute-start | bytes 1671176 | tf_op jit(solution)/shard_map/ppermute | solution.py:373
  38.8 0.0 collective-permute-done.refs_1_
  38.8 6.0 %shard_map.85 = (bf16[8,256,128]{2,1,0:T(8,128)(2,1)}, f32[1,1,128]{2,1,0:T(1,128)S(1)}) custom-call(bf16[8,16,128]{2,1,0:T(8,128)(2,1)S(1)} %slice.17.own_seg, bf16[8,16,128]{2,1,0:T(8,128)(2,1)S(1)} %slice.19.other_seg, bf16[8,256,128]{2,1,0:T(8,128)(2,1)S(1)} %slice.20.rows_slab.refs_0_, bf16[8,272,128]{2,1,0:T(8,128)(2,1)S(1)} %slice.18.refs_0_.rows_slab, ...), custom_call_target="tpu_custom_call" | custom-call | flops 2147483648 | bytes 2097152 | tf_op jit(solution)/shard_map/pallas_call | solution.py:325
  44.8 6.6 %all-to-all-start.2 = ((bf16[8,256,128]{2,1,0:T(8,128)(2,1)}), bf16[8,256,128]{2,1,0:T(8,128)(2,1)S(1)}, u32[]{:S(2)}, u32[]{:S(2)}) async-start(bf16[8,256,128]{2,1,0:T(8,128)(2,1)} %get-tuple-element.11), calls=%async_computation.2 | async-start | bytes 1048576 | tf_op jit(solution)/shard_map/all_to_all | solution.py:359
  51.4 0.0 collective-permute-done.1.other.refs_1_
  51.4 0.5 collective-permute-done.2
  51.9 1.2 %collective-permute-start.3 = (bf16[8,272,128]{2,1,0:T(8,128)(2,1)S(1)}, bf16[8,272,128]{2,1,0:T(8,128)(2,1)S(1)}, u32[]{:S(2)}, u32[]{:S(2)}) collective-permute-start(bf16[8,272,128]{2,1,0:T(8,128)(2,1)S(1)} %broadcast_add_fusion.refs_2_), channel_id=1, source_target_pairs={{0,4},{4,0},{1,5},{5,1},{2,6},{6,2},{3,7},{7,3},{8,12},{12,8},{9,1... | collective-permute-start | bytes 1671176 | tf_op jit(solution)/shard_map/ppermute | solution.py:369
  53.1 1.6 %collective-permute-done.3.refs_3_ = bf16[8,272,128]{2,1,0:T(8,128)(2,1)S(1)} collective-permute-done((bf16[8,272,128]{2,1,0:T(8,128)(2,1)S(1)}, bf16[8,272,128]{2,1,0:T(8,128)(2,1)S(1)}, u32[]{:S(2)}, u32[]{:S(2)}) %collective-permute-start.3) | collective-permute-done | bytes 557088 | tf_op jit(solution)/shard_map/ppermute | solution.py:369
  54.7 8.2 %shard_map.87 = bf16[8,256,128]{2,1,0:T(8,128)(2,1)} custom-call(bf16[8,16,128]{2,1,0:T(8,128)(2,1)S(1)} %slice.17.own_seg, bf16[8,16,128]{2,1,0:T(8,128)(2,1)S(1)} %slice.19.other_seg, bf16[8,272,128]{2,1,0:T(8,128)(2,1)S(1)} %slice.18.refs_0_.rows_slab, bf16[8,256,128]{2,1,0:T(8,128)(2,1)S(1)} %slice.20.rows_slab.refs_0_, ...), custom_call_target="tpu_custom_call" | custom-call | tf_op jit(solution)/shard_map/pallas_call | solution.py:325
  62.9 1.9 %all-to-all-done.2.back = bf16[8,256,128]{2,1,0:T(8,128)(2,1)S(1)} async-done(((bf16[8,256,128]{2,1,0:T(8,128)(2,1)}), bf16[8,256,128]{2,1,0:T(8,128)(2,1)S(1)}, u32[]{:S(2)}, u32[]{:S(2)}) %all-to-all-start.2) | async-done | bytes 524320 | tf_op jit(solution)/shard_map/all_to_all | solution.py:359
  64.8 6.0 %all-to-all-start.1 = ((bf16[8,256,128]{2,1,0:T(8,128)(2,1)}), bf16[8,256,128]{2,1,0:T(8,128)(2,1)S(1)}, u32[]{:S(2)}, u32[]{:S(2)}) async-start(bf16[8,256,128]{2,1,0:T(8,128)(2,1)} %shard_map.87), calls=%async_computation.1 | async-start | bytes 1048576 | tf_op jit(solution)/shard_map/all_to_all | solution.py:359
  70.8 0.9 %shard_map.88 = (bf16[128,1024]{1,0:T(8,128)(2,1)}, bf16[128,1024]{1,0:T(8,128)(2,1)}, bf16[128,1024]{1,0:T(8,128)(2,1)}, bf16[128,1024]{1,0:T(8,128)(2,1)}) custom-call(bf16[8,256,128]{2,1,0:T(8,128)(2,1)S(1)} %all-to-all-done.2.back), custom_call_target="tpu_custom_call" | custom-call | tf_op jit(solution)/shard_map/pallas_call | solution.py:126
  71.7 11.5 %all-to-all-done.1.back = bf16[8,256,128]{2,1,0:T(8,128)(2,1)S(1)} async-done(((bf16[8,256,128]{2,1,0:T(8,128)(2,1)}), bf16[8,256,128]{2,1,0:T(8,128)(2,1)S(1)}, u32[]{:S(2)}, u32[]{:S(2)}) %all-to-all-start.1) | async-done | bytes 524320 | tf_op jit(solution)/shard_map/all_to_all | solution.py:359
  83.2 0.9 %shard_map.89 = (bf16[128,1024]{1,0:T(8,128)(2,1)}, bf16[128,1024]{1,0:T(8,128)(2,1)}, bf16[128,1024]{1,0:T(8,128)(2,1)}, bf16[128,1024]{1,0:T(8,128)(2,1)}) custom-call(bf16[8,256,128]{2,1,0:T(8,128)(2,1)S(1)} %all-to-all-done.1.back, ...), custom_call_target="tpu_custom_call", output_to_operand_aliasing={{0}: (1, {}), {1}: (2, {}), {2}: (3, {}), {3}: (4, {})} | custom-call | tf_op jit(solution)/shard_map/pallas_call | solution.py:126
  (7 shorter events, 0.1 us)
Async XLA Ops:
  36.6 2.2 %collective-permute-start = (bf16[8,272,128]{2,1,0:T(8,128)(2,1)S(1)}, bf16[8,272,128]{2,1,0:T(8,128)(2,1)S(1)}, u32[]{:S(2)}, u32[]{:S(2)}) collective-permute-start(bf16[8,272,128]{2,1,0:T(8,128)(2,1)S(1)} %slice.18.refs_0_.rows_slab), channel_id=1, source_target_pairs={{0,4},{4,0},{1,5},{5,1},{2,6},{6,2},{3,7},{7,3},{8,12},{12,8},{9,1... | collective-permute-start | bytes 1671176 | tf_op jit(solution)/shard_map/ppermute | solution.py:369
  36.7 14.7 %collective-permute-start.1 = (bf16[8,256,128]{2,1,0:T(8,128)(2,1)S(1)}, bf16[8,256,128]{2,1,0:T(8,128)(2,1)S(1)}, u32[]{:S(2)}, u32[]{:S(2)}) collective-permute-start(bf16[8,256,128]{2,1,0:T(8,128)(2,1)S(1)} %slice.20.rows_slab.refs_0_), channel_id=1, source_target_pairs={{0,4},{4,0},{1,5},{5,1},{2,6},{6,2},{3,7},{7,3},{8,12},{12,8},{9,1... | collective-permute-start | bytes 1572872 | tf_op jit(solution)/shard_map/ppermute | solution.py:369
  37.2 14.6 %collective-permute-start.2 = (bf16[8,272,128]{2,1,0:T(8,128)(2,1)S(1)}, bf16[8,272,128]{2,1,0:T(8,128)(2,1)S(1)}, u32[]{:S(2)}, u32[]{:S(2)}) collective-permute-start(bf16[8,272,128]{2,1,0:T(8,128)(2,1)S(1)} %slice.18.refs_0_.rows_slab), channel_id=1, source_target_pairs={{0,16},{16,0},{1,17},{17,1},{2,18},{18,2},{3,19},{19,3},{4,20},{20... | collective-permute-start | bytes 1671176 | tf_op jit(solution)/shard_map/ppermute | solution.py:373
  44.8 20.0 %all-to-all-start.2 = ((bf16[8,256,128]{2,1,0:T(8,128)(2,1)}), bf16[8,256,128]{2,1,0:T(8,128)(2,1)S(1)}, u32[]{:S(2)}, u32[]{:S(2)}) async-start(bf16[8,256,128]{2,1,0:T(8,128)(2,1)} %get-tuple-element.11), calls=%async_computation.2 | async-start | bytes 1048576 | tf_op jit(solution)/shard_map/all_to_all | solution.py:359
  51.9 2.8 %collective-permute-start.3 = (bf16[8,272,128]{2,1,0:T(8,128)(2,1)S(1)}, bf16[8,272,128]{2,1,0:T(8,128)(2,1)S(1)}, u32[]{:S(2)}, u32[]{:S(2)}) collective-permute-start(bf16[8,272,128]{2,1,0:T(8,128)(2,1)S(1)} %broadcast_add_fusion.refs_2_), channel_id=1, source_target_pairs={{0,4},{4,0},{1,5},{5,1},{2,6},{6,2},{3,7},{7,3},{8,12},{12,8},{9,1... | collective-permute-start | bytes 1671176 | tf_op jit(solution)/shard_map/ppermute | solution.py:369
  64.8 18.4 %all-to-all-start.1 = ((bf16[8,256,128]{2,1,0:T(8,128)(2,1)}), bf16[8,256,128]{2,1,0:T(8,128)(2,1)S(1)}, u32[]{:S(2)}, u32[]{:S(2)}) async-start(bf16[8,256,128]{2,1,0:T(8,128)(2,1)} %shard_map.87), calls=%async_computation.1 | async-start | bytes 1048576 | tf_op jit(solution)/shard_map/all_to_all | solution.py:359

commit v2 on v1

--- a/solution.py
+++ b/solution.py
@@ -21,7 +21,8 @@
 DEVICE_AXES = ("sup", "pair", "core", "head")
 HEAD_AXES = ("head", "pair")
 SEG_ROWS = 16
-TAG_FLOPS = 40_000_000_000
+SECOND_FLOPS = 40_000_000_000
+OUTPUTS = {"first": ("packed", "tag"), "second": ("sums", "sums", "tag"), "last": ("packed",)}
 ATTEND_VMEM = 24 * 1024 * 1024
 MOVE_VMEM = 8 * 1024 * 1024
 PACK_VMEM = 63 * 1024 * 1024
@@ -32,6 +33,10 @@
         copy.start()
     for copy in copies:
         copy.wait()
+
+
+def listed(count):
+    return [(index + count // 2) % count for index in range(count)]
 
 
 def pack_kernel(queries, keys, values, out_grad, segment, packed, *scratch):
@@ -137,53 +142,41 @@
     )(back, *outs)
 
 
-def tag_kernel(given, other, tag):
-    tag[...] = given[...]
-
-
-def later_tag(tag, other):
-    vmem = pl.BlockSpec(memory_space=pltpu.VMEM)
-    return pl.pallas_call(
-        tag_kernel,
-        out_shape=jax.ShapeDtypeStruct(tag.shape, tag.dtype),
-        in_specs=[vmem, pl.BlockSpec(memory_space=pl.ANY)],
-        out_specs=vmem,
-        compiler_params=pltpu.CompilerParams(vmem_limit_bytes=MOVE_VMEM),
-        cost_estimate=pl.CostEstimate(
-            flops=TAG_FLOPS, bytes_accessed=2 * tag.size, transcendentals=0
-        ),
-    )(tag, other)
-
-
-def attend_kernel(factors, slabs, forward, own_seg, other_seg, rows_slab, *refs):
+def attend_kernel(factors, slabs, step_name, own_seg, other_seg, rows_slab, *refs):
     score_scale, norm = factors
-    col_slabs = refs[: 2 * slabs]
-    packed, *tag = refs[2 * slabs : -11]
+    forward, skipped = step_name == "first", 2 if step_name == "last" else 0
+    col_slabs, refs = refs[: 2 * slabs - skipped], refs[2 * slabs - skipped :]
+    given, outs = refs[: -11 - len(OUTPUTS[step_name])], refs[-11 - len(OUTPUTS[step_name]) : -11]
     seg, seg_rows, seg_cols, row_one, row_two, col_one, col_two = refs[-11:-4]
     sum_one, sum_two, work, sem = refs[-4:]
     parity, core = lax.axis_index("sup") % 2, lax.axis_index("core")
     sign = (1 - 2 * parity) * (1 if forward else -1)
     chunks = rows_slab.shape[0]
-    tokens = packed.shape[1] // 2
+    tokens = own_seg.shape[2]
     half_rows = chunks // PAIR * tokens
     half_blocks = half_rows // COLS
     local_blocks = REACH * half_blocks
     row_blocks = chunks * tokens // ROWS
     col_chunks = COLS // tokens
-    if tag:
-        tag[0][...] = jnp.zeros_like(tag[0])
+    first_block = local_blocks if skipped else 0
+    if step_name == "first":
+        outs[1][...] = jnp.zeros_like(outs[1])
+    if step_name == "second":
+        outs[2][...] = given[0][...]
 
     def place_of(index, chunk):
         slab, owner = index // 2, (core if index % 2 == 0 else 1 - core)
-        inner, pair = divmod(chunks - 1 - chunk, PAIR)
+        inner, pair = divmod(listed(chunks)[chunk], PAIR)
         return (slab * REACH + pair * CORE + owner) * (chunks // PAIR) + inner
 
     def row_of(chunk):
-        inner, pair = divmod(chunks - 1 - chunk, PAIR)
+        inner, pair = divmod(listed(chunks)[chunk], PAIR)
         return (pair * (chunks // PAIR) + inner) * tokens
 
-    for index, source in enumerate(col_slabs):
-        source, at = (source, 2 * tokens) if index > 1 else ((own_seg, other_seg)[index], 0)
+    for index in range(2 * slabs):
+        local = index < 2
+        source = (own_seg, other_seg)[index] if local else col_slabs[index - skipped]
+        at = 0 if local else 2 * tokens
         for chunk in range(chunks):
             numbers = source[chunk, pl.ds(at, SEG_ROWS)].astype(jnp.float32)[:1]
             place = place_of(index, chunk)
@@ -191,9 +184,9 @@
             seg_cols[place // col_chunks, :, lanes] = numbers.astype(jnp.int32)
     to_scalars = pltpu.make_async_copy(seg_cols, seg, sem)
     to_scalars.start()
-    for index, source in enumerate(col_slabs):
+    for index, source in enumerate(col_slabs, skipped):
         for chunk in range(chunks):
-            place = place_of(index, chunk)
+            place = place_of(index, chunk) - first_block * col_chunks
             rows = pl.ds(row_of(chunk) % COLS, tokens)
             for slot, ref in enumerate((col_one, col_two)):
                 ref[place // col_chunks, rows] = source[chunk, pl.ds(slot * tokens, tokens)]
@@ -212,8 +205,8 @@
     def seg_at(token):
         return seg[token // COLS, 0, token % COLS]
 
-    sum_one[...] = jnp.zeros_like(sum_one)
-    sum_two[...] = jnp.zeros_like(sum_two)
+    for index, ref in enumerate((sum_one, sum_two)):
+        ref[...] = given[index][...] if step_name == "last" else jnp.zeros_like(ref)
     to_scalars.wait()
     total = 0
     for row_block in range(row_blocks):
@@ -235,7 +228,7 @@
                     jnp.broadcast_to(numbers, (DH, tokens))
                 ).astype(jnp.int32)
 
-        for block in range(slabs * local_blocks):
+        for block in range(first_block, slabs * local_blocks):
             col_token = col_token_of(block)
             col_first, col_last = seg[block, 0, 0], seg[block, 0, COLS - 1]
             touching = (col_last >= row_first) & (col_first <= row_last)
@@ -261,6 +254,7 @@
 
     def tile(item, masked):
         row_block, block = work[0, item], work[1, item]
+        held = block - first_block
         if masked:
             offset = (col_token_of(block) - row_token_of(row_block)) * sign
             distance = (
@@ -270,7 +264,7 @@
         for part in range(0, ROWS, PART):
             at = pl.ds(pl.multiple_of(row_block * ROWS + part, PART), PART)
             scores, dprobs = [
-                lax.dot_general(rows[at], cols[block], dims, preferred_element_type=jnp.float32)
+                lax.dot_general(rows[at], cols[held], dims, preferred_element_type=jnp.float32)
                 for rows, cols in ((row_one, col_one), (row_two, col_two))
             ]
             weights, dscores = [], []
@@ -291,7 +285,7 @@
                 dscores.append(jnp.concatenate([piece[1] for piece in pieces], axis=1))
             for target, left, cols in ((sum_one, weights, col_two), (sum_two, dscores, col_one)):
                 target[row_block, pl.ds(part, PART)] += jnp.dot(
-                    jnp.concatenate(left, axis=0), cols[block], preferred_element_type=jnp.float32
+                    jnp.concatenate(left, axis=0), cols[held], preferred_element_type=jnp.float32
                 )
 
     def step(item, carry):
@@ -301,6 +295,11 @@
         return carry
 
     lax.fori_loop(0, total, step, 0)
+    if step_name == "second":
+        outs[0][...] = sum_one[...]
+        outs[1][...] = sum_two[...]
+        return
+    packed = outs[0]
     for chunk in range(chunks):
         row_block, inner = row_of(chunk) // ROWS, row_of(chunk) % ROWS
         at = pl.ds(inner, tokens)
@@ -310,31 +309,37 @@
         ).astype(packed.dtype)
 
 
-def attend(forward, rows_slab, col_slabs, local_segs):
+def attend(step_name, rows_slab, col_slabs, local_segs, given=()):
     chunks = rows_slab.shape[0]
     rows = chunks * DH
-    slabs = len(col_slabs) // 2
+    skipped = 2 if step_name == "last" else 0
+    slabs = (len(col_slabs) + skipped) // 2
     reach = CORE * rows
     factors = (1.0 / math.sqrt(DH), 1.0 / math.sqrt(reach))
     vmem = pl.BlockSpec(memory_space=pltpu.VMEM)
     dtype = rows_slab.dtype
     blocks = slabs * reach // COLS
     row_blocks = rows // ROWS
-    sums = jax.ShapeDtypeStruct((chunks, 2 * rows // chunks, DH), dtype)
-    tag = [jax.ShapeDtypeStruct((1, 1, DH), jnp.float32)] if forward else []
+    outputs = {
+        "packed": jax.ShapeDtypeStruct((chunks, 2 * rows // chunks, DH), dtype),
+        "sums": jax.ShapeDtypeStruct((row_blocks, ROWS, DH), jnp.float32),
+        "tag": jax.ShapeDtypeStruct((1, 1, DH), jnp.float32),
+    }
+    outputs = [outputs[name] for name in OUTPUTS[step_name]]
+    flops = {"first": 8 * DH * rows * reach * slabs, "second": SECOND_FLOPS, "last": 0}[step_name]
     return pl.pallas_call(
-        functools.partial(attend_kernel, factors, slabs, forward),
-        out_shape=[sums] + tag,
-        in_specs=[vmem] * (3 + 2 * slabs),
-        out_specs=[vmem] * (1 + len(tag)),
+        functools.partial(attend_kernel, factors, slabs, step_name),
+        out_shape=outputs,
+        in_specs=[vmem] * (3 + len(col_slabs) + len(given)),
+        out_specs=[vmem] * len(outputs),
         scratch_shapes=[
             pltpu.SMEM((blocks, 1, COLS), jnp.int32),
             pltpu.VMEM((rows, DH), jnp.int32),
             pltpu.VMEM((blocks, 1, COLS), jnp.int32),
             pltpu.VMEM((rows, DH), dtype),
             pltpu.VMEM((rows, DH), dtype),
-            pltpu.VMEM((blocks, COLS, DH), dtype),
-            pltpu.VMEM((blocks, COLS, DH), dtype),
+            pltpu.VMEM((len(col_slabs) * rows // COLS, COLS, DH), dtype),
+            pltpu.VMEM((len(col_slabs) * rows // COLS, COLS, DH), dtype),
         ]
         + [
             pltpu.VMEM((row_blocks, ROWS, DH), jnp.float32),
@@ -343,12 +348,8 @@
             pltpu.SemaphoreType.DMA(()),
         ],
         compiler_params=pltpu.CompilerParams(vmem_limit_bytes=ATTEND_VMEM),
-        cost_estimate=pl.CostEstimate(
-            flops=8 * DH * rows * reach * slabs if forward else 0,
-            bytes_accessed=8 * rows_slab.size if forward else 0,
-            transcendentals=rows * reach * slabs if forward else 0,
-        ),
-    )(*local_segs, rows_slab, *col_slabs)
+        cost_estimate=pl.CostEstimate(flops=flops, bytes_accessed=0, transcendentals=0),
+    )(*local_segs, rows_slab, *col_slabs, *given)
 
 
 def shards(queries, keys, values, out_grad, segment):
@@ -361,7 +362,7 @@
             HEAD_AXES,
             split_axis=0,
             concat_axis=0,
-            axis_index_groups=[list(range(packed.shape[0]))[::-1]],
+            axis_index_groups=[listed(packed.shape[0])],
             tiled=True,
         )
 
@@ -382,10 +383,11 @@
     if sups > 2:
         later = over_sups(jnp.concatenate([second_own, local_segs[0]], axis=1), 1)
         first_all = first_cols + with_other_core(later)
-    first_sums, tag = attend(True, second_own, first_all, local_segs)
+    first_sums, tag = attend("first", second_own, first_all, local_segs)
     first_back = over_heads(first_sums)
-    beyond_cols = with_other_core(beyond + later_tag(tag, second_cols[1]).astype(beyond.dtype))
-    (second_sums,) = attend(False, first_own, second_cols + beyond_cols, local_segs)
+    *local_sums, tag = attend("second", first_own, second_cols, local_segs, (tag,))
+    beyond_cols = with_other_core(beyond + tag.astype(beyond.dtype))
+    (second_sums,) = attend("last", first_own, beyond_cols, local_segs, local_sums)
     second_back = over_heads(second_sums)
     return tuple(unpack(1, second_back, unpack(0, first_back)))
 

time: 84.6 us -> 80.5 us (0.952)
  starting transfers between devices: 16 us -> 13.1 us
  blocking collectives: 33.8 us -> 32.7 us
  Pallas kernels: 18 us -> 19 us
  waiting for transfers between devices: 15.4 us -> 14.4 us
    all_to_all x2, starting transfers between devices: 12.6 us -> 10.9 us  [over_heads(): lax.all_to_all(packed, HEAD_AXES, split_axis=0, concat_axis=0, axis_index...]
    ppermute x3, starting transfers between devices: 1.86 us -> 0.7 us  [with_other_core(): return [slab, lax.ppermute(slab, 'core', [(0, 1), (1, 0)])]]
    all_to_all x1, blocking collectives: 33.8 us -> 32.7 us  [over_heads(): lax.all_to_all(packed, HEAD_AXES, split_axis=0, concat_axis=0, axis_index...]
    pallas_call x3, Pallas kernels: 14.1 us -> 15.1 us  [attend(): pl.pallas_call(functools.partial(attend_kernel, factors, slabs, step_name...]
    all_to_all x2, waiting for transfers between devices: 13.4 us -> 12.5 us  [over_heads(): lax.all_to_all(packed, HEAD_AXES, split_axis=0, concat_axis=0, axis_index...]
  transfers between devices with their start and end apart: 6 -> 6, of which waited for: 4 -> 3; matrix products, arithmetic and copies ran while one was open for 0% -> 0% of each run, Pallas kernels for 18% -> 20%
where the time goes in v2:
time: 80.5 us; the launch traced here: 80.1 us
  blocking collectives  32.7 us (41%)
  Pallas kernels  19 us (24%)
  waiting for transfers between devices  14.4 us (18%)
  starting transfers between devices  13.1 us (16%)
    all_to_all x1, blocking collectives, over_heads(): lax.all_to_all(packed, HEAD_AXES, split_axis=0, concat_axis=0, axis_index...  32.7 us
    pallas_call x3, Pallas kernels, attend(): pl.pallas_call(functools.partial(attend_kernel, factors, slabs, step_name...  15.1 us
    all_to_all x2, waiting for transfers between devices, over_heads(): lax.all_to_all(packed, HEAD_AXES, split_axis=0, concat_axis=0, axis_index...  12.5 us
    all_to_all x2, starting transfers between devices, over_heads(): lax.all_to_all(packed, HEAD_AXES, split_axis=0, concat_axis=0, axis_index...  10.9 us
    pallas_call x1, Pallas kernels, pack(): pl.pallas_call(pack_kernel, out_shape=jax.ShapeDtypeStruct(shape, queries...  2.09 us
    ppermute x3, waiting for transfers between devices, with_other_core(): return [slab, lax.ppermute(slab, 'core', [(0, 1), (1, 0)])]  1.95 us
    pallas_call x2, Pallas kernels, unpack(): pl.pallas_call(functools.partial(unpack_kernel, queries_on), out_shape=[j...  1.77 us
  transfers between devices with their start and end apart: 6, of which 3 were waited for; matrix products, arithmetic and copies ran while one was open for 0% of the time, Pallas kernels for 20%

profile of v2, /device:TPU:0, one launch (start us, length us, event | category | flops | bytes accessed | tf_op | source)
XLA Modules:
  0.0 80.1 jit_solution(14513076134174802460)
XLA Ops:
  0.6 2.1 %shard_map.84 = bf16[8,528,128]{2,1,0:T(8,128)(2,1)} custom-call(bf16[128,1024]{1,0:T(8,128)(2,1)} %queries.1, bf16[128,1024]{1,0:T(8,128)(2,1)} %keys.1, bf16[128,1024]{1,0:T(8,128)(2,1)} %values.1, bf16[128,1024]{1,0:T(8,128)(2,1)} %out_grad.1, s32[1,128]{1,0:T(1,128)} %bitcast.3), custom_call_target="tpu_custom_call" | custom-call | tf_op jit(solution)/shard_map/pallas_call | solution.py:94
  2.7 32.7 %all_to_all.15 = bf16[8,528,128]{2,1,0:T(8,128)(2,1)S(1)} all-to-all(bf16[8,528,128]{2,1,0:T(8,128)(2,1)} %shard_map.84), channel_id=1, replica_groups={{2,10,3,11,0,8,1,9},{6,14,7,15,4,12,5,13},{18,26,19,27,16,24,17,25},{22..., dimensions={0} | all-to-all | bytes 2162688 | tf_op jit(solution)/shard_map/all_to_all | solution.py:360
  35.5 0.1 collective-permute-start
  35.6 0.6 collective-permute-start.2
  36.1 1.5 %collective-permute-start.1 = (bf16[8,272,128]{2,1,0:T(8,128)(2,1)S(1)}, bf16[8,272,128]{2,1,0:T(8,128)(2,1)S(1)}, u32[]{:S(2)}, u32[]{:S(2)}) collective-permute-start(bf16[8,272,128]{2,1,0:T(8,128)(2,1)S(1)} %slice.18.refs_0_.rows_slab), channel_id=1, source_target_pairs={{0,16},{16,0},{1,17},{17,1},{2,18},{18,2},{3,19},{19,3},{4,20},{20... | collective-permute-start | bytes 1671176 | tf_op jit(solution)/shard_map/ppermute | solution.py:374
  37.7 0.0 collective-permute-done.refs_1_
  37.7 6.0 %shard_map.85 = (bf16[8,256,128]{2,1,0:T(8,128)(2,1)}, f32[1,1,128]{2,1,0:T(1,128)S(1)}) custom-call(bf16[8,16,128]{2,1,0:T(8,128)(2,1)S(1)} %slice.17.own_seg, bf16[8,16,128]{2,1,0:T(8,128)(2,1)S(1)} %slice.19.other_seg, bf16[8,256,128]{2,1,0:T(8,128)(2,1)S(1)} %slice.20.rows_slab.refs_0_, bf16[8,272,128]{2,1,0:T(8,128)(2,1)S(1)} %slice.18.refs_0_.rows_slab, ...), custom_call_target="tpu_custom_call" | custom-call | flops 2147483648 | tf_op jit(solution)/shard_map/pallas_call | solution.py:330
  43.7 4.9 %all-to-all-start.2 = ((bf16[8,256,128]{2,1,0:T(8,128)(2,1)}), bf16[8,256,128]{2,1,0:T(8,128)(2,1)S(1)}, u32[]{:S(2)}, u32[]{:S(2)}) async-start(bf16[8,256,128]{2,1,0:T(8,128)(2,1)} %get-tuple-element.17), calls=%async_computation.2 | async-start | bytes 1048576 | tf_op jit(solution)/shard_map/all_to_all | solution.py:360
  48.6 0.0 collective-permute-done.2.refs_1_
  48.6 7.2 %shard_map.86 = (f32[2,512,128]{2,1,0:T(8,128)S(1)}, f32[2,512,128]{2,1,0:T(8,128)S(1)}, f32[1,1,128]{2,1,0:T(1,128)S(1)}) custom-call(bf16[8,16,128]{2,1,0:T(8,128)(2,1)S(1)} %slice.17.own_seg, bf16[8,16,128]{2,1,0:T(8,128)(2,1)S(1)} %slice.19.other_seg, bf16[8,272,128]{2,1,0:T(8,128)(2,1)S(1)} %slice.18.refs_0_.rows_slab, ...), custom_call_target="tpu_custom_call" | custom-call | flops 40000000000 | tf_op jit(solution)/shard_map/pallas_call | solution.py:330
  55.9 0.0 collective-permute-done.1
  55.9 0.1 collective-permute-start.3
  56.0 1.9 %collective-permute-done.3.refs_1_ = bf16[8,272,128]{2,1,0:T(8,128)(2,1)S(1)} collective-permute-done((bf16[8,272,128]{2,1,0:T(8,128)(2,1)S(1)}, bf16[8,272,128]{2,1,0:T(8,128)(2,1)S(1)}, u32[]{:S(2)}, u32[]{:S(2)}) %collective-permute-start.3) | collective-permute-done | bytes 557088 | tf_op jit(solution)/shard_map/ppermute | solution.py:370
  58.0 1.9 %shard_map.87 = bf16[8,256,128]{2,1,0:T(8,128)(2,1)} custom-call(bf16[8,16,128]{2,1,0:T(8,128)(2,1)S(1)} %slice.17.own_seg, bf16[8,16,128]{2,1,0:T(8,128)(2,1)S(1)} %slice.19.other_seg, bf16[8,272,128]{2,1,0:T(8,128)(2,1)S(1)} %slice.18.refs_0_.rows_slab, bf16[8,272,128]{2,1,0:T(8,128)(2,1)S(1)} %broadcast_add_fusion.refs_0_, ...), custom_call_target="tpu_custom_call" | custom-call | tf_op jit(solution)/shard_map/pallas_call | solution.py:330
  59.9 0.5 all-to-all-done.2.back
  60.4 6.0 %all-to-all-start.1 = ((bf16[8,256,128]{2,1,0:T(8,128)(2,1)}), bf16[8,256,128]{2,1,0:T(8,128)(2,1)S(1)}, u32[]{:S(2)}, u32[]{:S(2)}) async-start(bf16[8,256,128]{2,1,0:T(8,128)(2,1)} %shard_map.87), calls=%async_computation.1 | async-start | bytes 1048576 | tf_op jit(solution)/shard_map/all_to_all | solution.py:360
  66.3 0.9 %shard_map.88 = (bf16[128,1024]{1,0:T(8,128)(2,1)}, bf16[128,1024]{1,0:T(8,128)(2,1)}, bf16[128,1024]{1,0:T(8,128)(2,1)}, bf16[128,1024]{1,0:T(8,128)(2,1)}) custom-call(bf16[8,256,128]{2,1,0:T(8,128)(2,1)S(1)} %all-to-all-done.2.back), custom_call_target="tpu_custom_call" | custom-call | tf_op jit(solution)/shard_map/pallas_call | solution.py:131
  67.2 12.0 %all-to-all-done.1.back = bf16[8,256,128]{2,1,0:T(8,128)(2,1)S(1)} async-done(((bf16[8,256,128]{2,1,0:T(8,128)(2,1)}), bf16[8,256,128]{2,1,0:T(8,128)(2,1)S(1)}, u32[]{:S(2)}, u32[]{:S(2)}) %all-to-all-start.1) | async-done | bytes 524320 | tf_op jit(solution)/shard_map/all_to_all | solution.py:360
  79.2 0.9 %shard_map.89 = (bf16[128,1024]{1,0:T(8,128)(2,1)}, bf16[128,1024]{1,0:T(8,128)(2,1)}, bf16[128,1024]{1,0:T(8,128)(2,1)}, bf16[128,1024]{1,0:T(8,128)(2,1)}) custom-call(bf16[8,256,128]{2,1,0:T(8,128)(2,1)S(1)} %all-to-all-done.1.back, ...), custom_call_target="tpu_custom_call", output_to_operand_aliasing={{0}: (1, {}), {1}: (2, {}), {2}: (3, {}), {3}: (4, {})} | custom-call | tf_op jit(solution)/shard_map/pallas_call | solution.py:131
  (6 shorter events, 0.1 us)
Async XLA Ops:
  35.5 2.2 %collective-permute-start = (bf16[8,272,128]{2,1,0:T(8,128)(2,1)S(1)}, bf16[8,272,128]{2,1,0:T(8,128)(2,1)S(1)}, u32[]{:S(2)}, u32[]{:S(2)}) collective-permute-start(bf16[8,272,128]{2,1,0:T(8,128)(2,1)S(1)} %slice.18.refs_0_.rows_slab), channel_id=1, source_target_pairs={{0,4},{4,0},{1,5},{5,1},{2,6},{6,2},{3,7},{7,3},{8,12},{12,8},{9,1... | collective-permute-start | bytes 1671176 | tf_op jit(solution)/shard_map/ppermute | solution.py:370
  35.6 13.0 %collective-permute-start.2 = (bf16[8,256,128]{2,1,0:T(8,128)(2,1)S(1)}, bf16[8,256,128]{2,1,0:T(8,128)(2,1)S(1)}, u32[]{:S(2)}, u32[]{:S(2)}) collective-permute-start(bf16[8,256,128]{2,1,0:T(8,128)(2,1)S(1)} %slice.20.rows_slab.refs_0_), channel_id=1, source_target_pairs={{0,4},{4,0},{1,5},{5,1},{2,6},{6,2},{3,7},{7,3},{8,12},{12,8},{9,1... | collective-permute-start | bytes 1572872 | tf_op jit(solution)/shard_map/ppermute | solution.py:370
  36.1 19.7 %collective-permute-start.1 = (bf16[8,272,128]{2,1,0:T(8,128)(2,1)S(1)}, bf16[8,272,128]{2,1,0:T(8,128)(2,1)S(1)}, u32[]{:S(2)}, u32[]{:S(2)}) collective-permute-start(bf16[8,272,128]{2,1,0:T(8,128)(2,1)S(1)} %slice.18.refs_0_.rows_slab), channel_id=1, source_target_pairs={{0,16},{16,0},{1,17},{17,1},{2,18},{18,2},{3,19},{19,3},{4,20},{20... | collective-permute-start | bytes 1671176 | tf_op jit(solution)/shard_map/ppermute | solution.py:374
  43.7 16.7 %all-to-all-start.2 = ((bf16[8,256,128]{2,1,0:T(8,128)(2,1)}), bf16[8,256,128]{2,1,0:T(8,128)(2,1)S(1)}, u32[]{:S(2)}, u32[]{:S(2)}) async-start(bf16[8,256,128]{2,1,0:T(8,128)(2,1)} %get-tuple-element.17), calls=%async_computation.2 | async-start | bytes 1048576 | tf_op jit(solution)/shard_map/all_to_all | solution.py:360
  55.9 2.0 %collective-permute-start.3 = (bf16[8,272,128]{2,1,0:T(8,128)(2,1)S(1)}, bf16[8,272,128]{2,1,0:T(8,128)(2,1)S(1)}, u32[]{:S(2)}, u32[]{:S(2)}) collective-permute-start(bf16[8,272,128]{2,1,0:T(8,128)(2,1)S(1)} %broadcast_add_fusion.refs_0_), channel_id=1, source_target_pairs={{0,4},{4,0},{1,5},{5,1},{2,6},{6,2},{3,7},{7,3},{8,12},{12,8},{9,1... | collective-permute-start | bytes 1671176 | tf_op jit(solution)/shard_map/ppermute | solution.py:370
  60.4 18.9 %all-to-all-start.1 = ((bf16[8,256,128]{2,1,0:T(8,128)(2,1)}), bf16[8,256,128]{2,1,0:T(8,128)(2,1)S(1)}, u32[]{:S(2)}, u32[]{:S(2)}) async-start(bf16[8,256,128]{2,1,0:T(8,128)(2,1)} %shard_map.87), calls=%async_computation.1 | async-start | bytes 1048576 | tf_op jit(solution)/shard_map/all_to_all | solution.py:360

commit v3 on v2

--- a/solution.py
+++ b/solution.py
@@ -36,7 +36,8 @@
 
 
 def listed(count):
-    return [(index + count // 2) % count for index in range(count)]
+    middle = range(count // 2, count // 2 + PAIR)
+    return [*middle, *(index for index in range(count) if index not in middle)]
 
 
 def pack_kernel(queries, keys, values, out_grad, segment, packed, *scratch):

time: 80.5 us -> 79.8 us (level); the launches traced: 80.1 us -> 78.3 us
  waiting for transfers between devices: 14.4 us -> 12.3 us
    all_to_all x2, waiting for transfers between devices: 12.5 us -> 10.4 us  [over_heads(): lax.all_to_all(packed, HEAD_AXES, split_axis=0, concat_axis=0, axis_index...]
  transfers between devices with their start and end apart: 6 -> 6, of which waited for: 3 -> 2; matrix products, arithmetic and copies ran while one was open for 0% -> 0% of each run, Pallas kernels for 20% -> 21%
where the time goes in v3:
time: 79.8 us; the launch traced here: 78.3 us
  blocking collectives  32.8 us (41%)
  Pallas kernels  19.6 us (25%)
  starting transfers between devices  12.7 us (16%)
  waiting for transfers between devices  12.3 us (15%)
    all_to_all x1, blocking collectives, over_heads(): lax.all_to_all(packed, HEAD_AXES, split_axis=0, concat_axis=0, axis_index...  32.8 us
    pallas_call x3, Pallas kernels, attend(): pl.pallas_call(functools.partial(attend_kernel, factors, slabs, step_name...  15.7 us
    all_to_all x2, starting transfers between devices, over_heads(): lax.all_to_all(packed, HEAD_AXES, split_axis=0, concat_axis=0, axis_index...  10.5 us
    all_to_all x2, waiting for transfers between devices, over_heads(): lax.all_to_all(packed, HEAD_AXES, split_axis=0, concat_axis=0, axis_index...  10.4 us
    pallas_call x1, Pallas kernels, pack(): pl.pallas_call(pack_kernel, out_shape=jax.ShapeDtypeStruct(shape, queries...  2.09 us
    ppermute x3, waiting for transfers between devices, with_other_core(): return [slab, lax.ppermute(slab, 'core', [(0, 1), (1, 0)])]  1.95 us
    pallas_call x2, Pallas kernels, unpack(): pl.pallas_call(functools.partial(unpack_kernel, queries_on), out_shape=[j...  1.77 us
  transfers between devices with their start and end apart: 6, of which 2 were waited for; matrix products, arithmetic and copies ran while one was open for 0% of the time, Pallas kernels for 21%

profile of v3, /device:TPU:0, one launch (start us, length us, event | category | flops | bytes accessed | tf_op | source)
XLA Modules:
  0.0 78.3 jit_solution(8551856049874710113)
XLA Ops:
  0.6 2.1 %shard_map.84 = bf16[8,528,128]{2,1,0:T(8,128)(2,1)} custom-call(bf16[128,1024]{1,0:T(8,128)(2,1)} %queries.1, bf16[128,1024]{1,0:T(8,128)(2,1)} %keys.1, bf16[128,1024]{1,0:T(8,128)(2,1)} %values.1, bf16[128,1024]{1,0:T(8,128)(2,1)} %out_grad.1, s32[1,128]{1,0:T(1,128)} %bitcast.3), custom_call_target="tpu_custom_call" | custom-call | tf_op jit(solution)/shard_map/pallas_call | solution.py:95
  2.7 32.8 %all_to_all.15 = bf16[8,528,128]{2,1,0:T(8,128)(2,1)S(1)} all-to-all(bf16[8,528,128]{2,1,0:T(8,128)(2,1)} %shard_map.84), channel_id=1, replica_groups={{2,10,0,8,1,9,3,11},{6,14,4,12,5,13,7,15},{18,26,16,24,17,25,19,27},{22..., dimensions={0} | all-to-all | bytes 2162688 | tf_op jit(solution)/shard_map/all_to_all | solution.py:361
  35.6 0.1 collective-permute-start
  35.7 0.6 collective-permute-start.2
  36.2 1.5 %collective-permute-start.1 = (bf16[8,272,128]{2,1,0:T(8,128)(2,1)S(1)}, bf16[8,272,128]{2,1,0:T(8,128)(2,1)S(1)}, u32[]{:S(2)}, u32[]{:S(2)}) collective-permute-start(bf16[8,272,128]{2,1,0:T(8,128)(2,1)S(1)} %slice.18.refs_0_.rows_slab), channel_id=1, source_target_pairs={{0,16},{16,0},{1,17},{17,1},{2,18},{18,2},{3,19},{19,3},{4,20},{20... | collective-permute-start | bytes 1671176 | tf_op jit(solution)/shard_map/ppermute | solution.py:375
  37.8 0.0 collective-permute-done.refs_1_
  37.8 6.2 %shard_map.85 = (bf16[8,256,128]{2,1,0:T(8,128)(2,1)}, f32[1,1,128]{2,1,0:T(1,128)S(1)}) custom-call(bf16[8,16,128]{2,1,0:T(8,128)(2,1)S(1)} %slice.17.own_seg, bf16[8,16,128]{2,1,0:T(8,128)(2,1)S(1)} %slice.19.other_seg, bf16[8,256,128]{2,1,0:T(8,128)(2,1)S(1)} %slice.20.rows_slab.refs_0_, bf16[8,272,128]{2,1,0:T(8,128)(2,1)S(1)} %slice.18.refs_0_.rows_slab, ...), custom_call_target="tpu_custom_call" | custom-call | flops 2147483648 | tf_op jit(solution)/shard_map/pallas_call | solution.py:331
  44.0 4.8 %all-to-all-start.2 = ((bf16[8,256,128]{2,1,0:T(8,128)(2,1)}), bf16[8,256,128]{2,1,0:T(8,128)(2,1)S(1)}, u32[]{:S(2)}, u32[]{:S(2)}) async-start(bf16[8,256,128]{2,1,0:T(8,128)(2,1)} %get-tuple-element.17), calls=%async_computation.2 | async-start | bytes 1048576 | tf_op jit(solution)/shard_map/all_to_all | solution.py:361
  48.7 0.0 collective-permute-done.2.refs_1_
  48.7 7.5 %shard_map.86 = (f32[2,512,128]{2,1,0:T(8,128)S(1)}, f32[2,512,128]{2,1,0:T(8,128)S(1)}, f32[1,1,128]{2,1,0:T(1,128)S(1)}) custom-call(bf16[8,16,128]{2,1,0:T(8,128)(2,1)S(1)} %slice.17.own_seg, bf16[8,16,128]{2,1,0:T(8,128)(2,1)S(1)} %slice.19.other_seg, bf16[8,272,128]{2,1,0:T(8,128)(2,1)S(1)} %slice.18.refs_0_.rows_slab, ...), custom_call_target="tpu_custom_call" | custom-call | flops 40000000000 | tf_op jit(solution)/shard_map/pallas_call | solution.py:331
  56.3 0.0 collective-permute-done.1
  56.4 0.1 collective-permute-start.3
  56.4 1.9 %collective-permute-done.3.refs_1_ = bf16[8,272,128]{2,1,0:T(8,128)(2,1)S(1)} collective-permute-done((bf16[8,272,128]{2,1,0:T(8,128)(2,1)S(1)}, bf16[8,272,128]{2,1,0:T(8,128)(2,1)S(1)}, u32[]{:S(2)}, u32[]{:S(2)}) %collective-permute-start.3) | collective-permute-done | bytes 557088 | tf_op jit(solution)/shard_map/ppermute | solution.py:371
  58.4 2.0 %shard_map.87 = bf16[8,256,128]{2,1,0:T(8,128)(2,1)} custom-call(bf16[8,16,128]{2,1,0:T(8,128)(2,1)S(1)} %slice.17.own_seg, bf16[8,16,128]{2,1,0:T(8,128)(2,1)S(1)} %slice.19.other_seg, bf16[8,272,128]{2,1,0:T(8,128)(2,1)S(1)} %slice.18.refs_0_.rows_slab, bf16[8,272,128]{2,1,0:T(8,128)(2,1)S(1)} %broadcast_add_fusion.refs_0_, ...), custom_call_target="tpu_custom_call" | custom-call | tf_op jit(solution)/shard_map/pallas_call | solution.py:331
  60.4 0.0 all-to-all-done.2.back
  60.4 5.7 %all-to-all-start.1 = ((bf16[8,256,128]{2,1,0:T(8,128)(2,1)}), bf16[8,256,128]{2,1,0:T(8,128)(2,1)S(1)}, u32[]{:S(2)}, u32[]{:S(2)}) async-start(bf16[8,256,128]{2,1,0:T(8,128)(2,1)} %shard_map.87), calls=%async_computation.1 | async-start | bytes 1048576 | tf_op jit(solution)/shard_map/all_to_all | solution.py:361
  66.2 0.9 %shard_map.88 = (bf16[128,1024]{1,0:T(8,128)(2,1)}, bf16[128,1024]{1,0:T(8,128)(2,1)}, bf16[128,1024]{1,0:T(8,128)(2,1)}, bf16[128,1024]{1,0:T(8,128)(2,1)}) custom-call(bf16[8,256,128]{2,1,0:T(8,128)(2,1)S(1)} %all-to-all-done.2.back), custom_call_target="tpu_custom_call" | custom-call | tf_op jit(solution)/shard_map/pallas_call | solution.py:132
  67.1 10.4 %all-to-all-done.1.back = bf16[8,256,128]{2,1,0:T(8,128)(2,1)S(1)} async-done(((bf16[8,256,128]{2,1,0:T(8,128)(2,1)}), bf16[8,256,128]{2,1,0:T(8,128)(2,1)S(1)}, u32[]{:S(2)}, u32[]{:S(2)}) %all-to-all-start.1) | async-done | bytes 524320 | tf_op jit(solution)/shard_map/all_to_all | solution.py:361
  77.4 0.9 %shard_map.89 = (bf16[128,1024]{1,0:T(8,128)(2,1)}, bf16[128,1024]{1,0:T(8,128)(2,1)}, bf16[128,1024]{1,0:T(8,128)(2,1)}, bf16[128,1024]{1,0:T(8,128)(2,1)}) custom-call(bf16[8,256,128]{2,1,0:T(8,128)(2,1)S(1)} %all-to-all-done.1.back, ...), custom_call_target="tpu_custom_call", output_to_operand_aliasing={{0}: (1, {}), {1}: (2, {}), {2}: (3, {}), {3}: (4, {})} | custom-call | tf_op jit(solution)/shard_map/pallas_call | solution.py:132
  (6 shorter events, 0.1 us)
Async XLA Ops:
  35.6 2.2 %collective-permute-start = (bf16[8,272,128]{2,1,0:T(8,128)(2,1)S(1)}, bf16[8,272,128]{2,1,0:T(8,128)(2,1)S(1)}, u32[]{:S(2)}, u32[]{:S(2)}) collective-permute-start(bf16[8,272,128]{2,1,0:T(8,128)(2,1)S(1)} %slice.18.refs_0_.rows_slab), channel_id=1, source_target_pairs={{0,4},{4,0},{1,5},{5,1},{2,6},{6,2},{3,7},{7,3},{8,12},{12,8},{9,1... | collective-permute-start | bytes 1671176 | tf_op jit(solution)/shard_map/ppermute | solution.py:371
  35.7 13.1 %collective-permute-start.2 = (bf16[8,256,128]{2,1,0:T(8,128)(2,1)S(1)}, bf16[8,256,128]{2,1,0:T(8,128)(2,1)S(1)}, u32[]{:S(2)}, u32[]{:S(2)}) collective-permute-start(bf16[8,256,128]{2,1,0:T(8,128)(2,1)S(1)} %slice.20.rows_slab.refs_0_), channel_id=1, source_target_pairs={{0,4},{4,0},{1,5},{5,1},{2,6},{6,2},{3,7},{7,3},{8,12},{12,8},{9,1... | collective-permute-start | bytes 1572872 | tf_op jit(solution)/shard_map/ppermute | solution.py:371
  36.2 20.1 %collective-permute-start.1 = (bf16[8,272,128]{2,1,0:T(8,128)(2,1)S(1)}, bf16[8,272,128]{2,1,0:T(8,128)(2,1)S(1)}, u32[]{:S(2)}, u32[]{:S(2)}) collective-permute-start(bf16[8,272,128]{2,1,0:T(8,128)(2,1)S(1)} %slice.18.refs_0_.rows_slab), channel_id=1, source_target_pairs={{0,16},{16,0},{1,17},{17,1},{2,18},{18,2},{3,19},{19,3},{4,20},{20... | collective-permute-start | bytes 1671176 | tf_op jit(solution)/shard_map/ppermute | solution.py:375
  44.0 16.5 %all-to-all-start.2 = ((bf16[8,256,128]{2,1,0:T(8,128)(2,1)}), bf16[8,256,128]{2,1,0:T(8,128)(2,1)S(1)}, u32[]{:S(2)}, u32[]{:S(2)}) async-start(bf16[8,256,128]{2,1,0:T(8,128)(2,1)} %get-tuple-element.17), calls=%async_computation.2 | async-start | bytes 1048576 | tf_op jit(solution)/shard_map/all_to_all | solution.py:361
  56.4 2.0 %collective-permute-start.3 = (bf16[8,272,128]{2,1,0:T(8,128)(2,1)S(1)}, bf16[8,272,128]{2,1,0:T(8,128)(2,1)S(1)}, u32[]{:S(2)}, u32[]{:S(2)}) collective-permute-start(bf16[8,272,128]{2,1,0:T(8,128)(2,1)S(1)} %broadcast_add_fusion.refs_0_), channel_id=1, source_target_pairs={{0,4},{4,0},{1,5},{5,1},{2,6},{6,2},{3,7},{7,3},{8,12},{12,8},{9,1... | collective-permute-start | bytes 1671176 | tf_op jit(solution)/shard_map/ppermute | solution.py:371
  60.4 17.0 %all-to-all-start.1 = ((bf16[8,256,128]{2,1,0:T(8,128)(2,1)}), bf16[8,256,128]{2,1,0:T(8,128)(2,1)S(1)}, u32[]{:S(2)}, u32[]{:S(2)}) async-start(bf16[8,256,128]{2,1,0:T(8,128)(2,1)} %shard_map.87), calls=%async_computation.1 | async-start | bytes 1048576 | tf_op jit(solution)/shard_map/all_to_all | solution.py:361
